TPU v7x, 128 devices: a whole 4x4x4 slice. The times are simulated.
128 devices in a mesh: gz: 32 (over z, x, y_hi), gy: 4 (over y_lo, core).
Axes of the slice: x: 4, y: 4 (y_hi: 2, y_lo: 2; y = y_hi * 2 + y_lo), z: 4, core: 2. Of those that a mesh axis runs over, the one named last changes fastest.
Arguments:
- features: bfloat16 [32, 64, 32, 256], P(None, 'gz', 'gy'), may hold values from -6 to 6
- w_enc: bfloat16 [27, 32, 32], replicated, may hold values from -0.21875 to 0.21875
- w_mid: bfloat16 [27, 64, 32], replicated, may hold values from -0.21875 to 0.21875
- w_dec: bfloat16 [27, 32, 96], replicated, may hold values from -0.125 to 0.125
- cotangent: bfloat16 [32, 64, 32, 256], P(None, 'gz', 'gy'), may hold values from -6 to 6
Outputs:
- decoded: bfloat16 [32, 64, 32, 256], P(None, 'gz', 'gy')
- grad_enc: float32 [27, 32, 32], replicated
- grad_mid: float32 [27, 64, 32], replicated
- grad_dec: float32 [27, 32, 96], replicated
All inputs are finite; a program needn't handle non-finite values.
Results may differ from a plain program's by a relative error of at most 0.013.
Values may be sent and summed in bfloat16 or wider, within the bound.
A program may use at most 128 MiB of HBM per device.

v0:
```python
import functools

import jax
import jax.numpy as jnp
from jax import lax
from jax.experimental import pallas as pl
from jax.experimental.pallas import tpu as pltpu
from jax.sharding import PartitionSpec as P

MESH = pl.DeviceIdType.MESH
BF = jnp.bfloat16
F32 = jnp.float32
DIRECTIONS = [(a, b) for a in (-1, 0, 1) for b in (-1, 0, 1) if (a, b) != (0, 0)]


def iota(shape, dim):
    return lax.broadcasted_iota(jnp.int32, shape, dim)


def hot(mask):
    return jnp.where(mask, 1.0, 0.0).astype(BF)


def dot(a, b):
    return jnp.dot(a, b, preferred_element_type=F32)


def dot_nt(a, b):
    return lax.dot_general(a, b, (((1,), (1,)), ((), ())), preferred_element_type=F32)


def rows_to_cells(chans, height):
    n = chans * height
    r, s = iota((n, n), 0), iota((n, n), 1)
    return hot(s == (r % chans) * height + r // chans)


def cells_to_rows(chans, height):
    n = chans * height
    r, s = iota((n, n), 0), iota((n, n), 1)
    return hot(r == (s % chans) * height + s // chans)


def split_four(width):
    half = width // 2
    r, s = iota((width, 2 * width), 0), iota((width, 2 * width), 1)
    return hot(r == 2 * (s % half) - 1 + s // half)


def shift_parity(width):
    half = width // 2
    r, s = iota((width, width), 0), iota((width, width), 1)
    c = s % half
    first = (s < half) & (c > 0) & (r == half + c - 1)
    second = (s >= half) & (c < half - 1) & (r == c + 1)
    return hot(first | second)


def shift_both(half):
    r, s = iota((half, 2 * half), 0), iota((half, 2 * half), 1)
    return hot(((s < half) & (r == s - 1)) | ((s >= half) & (r == s - half + 1)))


def merge_parity(width):
    half = width // 2
    r, s = iota((width, width), 0), iota((width, width), 1)
    return hot(s == 2 * (r % half) + r // half)


class Halo:
    def __init__(self, ref, send, recv, number, grid):
        self.ref, self.send, self.recv, self.number = ref, send, recv, number
        self.gz, self.gy, self.nz, self.ny = grid
        self.depth, self.height = ref.shape[0] - 2, ref.shape[1] - 2

    def exists(self, a, b):
        checks = []
        if a:
            checks.append(self.gz > 0 if a < 0 else self.gz < self.nz - 1)
        if b:
            checks.append(self.gy > 0 if b < 0 else self.gy < self.ny - 1)
        return functools.reduce(jnp.logical_and, checks)

    def source(self, d, n):
        return {-1: pl.ds(1, 1), 0: pl.ds(1, n), 1: pl.ds(n, 1)}[d]

    def target(self, d, n):
        return {-1: pl.ds(n + 1, 1), 0: pl.ds(1, n), 1: pl.ds(0, 1)}[d]

    def copy(self, i):
        a, b = DIRECTIONS[i]
        peer = (lax.rem(self.gz + a + self.nz, self.nz), lax.rem(self.gy + b + self.ny, self.ny))
        return pltpu.make_async_remote_copy(
            src_ref=self.ref.at[self.source(a, self.depth), self.source(b, self.height)],
            dst_ref=self.ref.at[self.target(a, self.depth), self.target(b, self.height)],
            send_sem=self.send.at[self.number, i],
            recv_sem=self.recv.at[self.number, i],
            device_id=peer,
            device_id_type=MESH,
        )

    def start(self):
        for i in (1, 6, 3, 4, 0, 2, 5, 7):
            pl.when(self.exists(*DIRECTIONS[i]))(lambda i=i: self.copy(i).start())

    def clear(self):
        for i, (a, b) in enumerate(DIRECTIONS):
            @pl.when(jnp.logical_not(self.exists(-a, -b)))
            def _(a=a, b=b):
                part = self.ref.at[self.target(a, self.depth), self.target(b, self.height)]
                part[...] = jnp.zeros(part.shape, part.dtype)

    def arrived(self):
        for i, (a, b) in enumerate(DIRECTIONS):
            pl.when(self.exists(-a, -b))(lambda i=i: self.copy(i).wait_recv())

    def sent(self):
        for i, (a, b) in enumerate(DIRECTIONS):
            pl.when(self.exists(a, b))(lambda i=i: self.copy(i).wait_send())


class Group:
    def __init__(self, size, me, peer):
        self.size, self.me, self.peer = size, me, peer

    def others(self):
        return [lax.rem(self.me + d, self.size) for d in range(1, self.size)]


class Total:
    def __init__(self, first, second, mine, one, two, whole, sems):
        self.first, self.second = first, second
        self.mine, self.one, self.two, self.whole = mine, one, two, whole
        self.send1, self.recv1, self.send2, self.recv2, self.send3, self.recv3 = sems

    def copy(self, src, dst, send, recv, slot, peer):
        return pltpu.make_async_remote_copy(
            src_ref=src, dst_ref=dst, send_sem=send, recv_sem=recv,
            device_id=peer, device_id_type=MESH,
        )

    def step1(self, t, incoming):
        g = self.first
        slot = t if incoming else g.me
        return self.copy(self.mine.at[t], self.one.at[slot], self.send1.at[t], self.recv1.at[slot], slot, g.peer(t))

    def step2(self, t, incoming):
        g = self.second
        slot = t if incoming else g.me
        return self.copy(self.two.at[g.me], self.two.at[slot], self.send2.at[t], self.recv2.at[slot], slot, g.peer(t))

    def step3(self, t, incoming):
        g = self.first
        slot = t if incoming else g.me
        return self.copy(self.whole.at[g.me], self.whole.at[slot], self.send3.at[t], self.recv3.at[slot], slot, g.peer(t))

    def start1(self):
        for t in self.first.others():
            self.step1(t, False).start()

    def start2(self):
        total = self.mine[self.first.me].astype(F32)
        for t in self.first.others():
            self.step1(t, True).wait_recv()
            total = total + self.one[t].astype(F32)
        self.two[self.second.me] = total.astype(BF)
        for t in self.second.others():
            self.step2(t, False).start()

    def start3(self):
        for t in self.second.others():
            self.step2(t, True).wait_recv()
        total = self.two[0].astype(F32)
        for t in range(1, self.second.size):
            total = total + self.two[t].astype(F32)
        self.whole[self.first.me] = total.astype(BF)
        for t in self.first.others():
            self.step3(t, False).start()

    def finish(self):
        for t in self.first.others():
            self.step3(t, True).wait_recv()

    def drain(self):
        for t in self.first.others():
            self.step1(t, False).wait_send()
            self.step3(t, False).wait_send()
        for t in self.second.others():
            self.step2(t, False).wait_send()


def pair(ref, z, y, step=1):
    a = ref[pl.ds(z, 3), pl.ds(y, 3)]
    b = ref[pl.ds(z, 3), pl.ds(y + step, 3)]
    rows = 9 * ref.shape[2]
    return jnp.concatenate([a.reshape(rows, ref.shape[3]), b.reshape(rows, ref.shape[3])], axis=1)


def silu_slope(value):
    sigma = 1.0 / (1.0 + jnp.exp(-value))
    return sigma * (1.0 + value * (1.0 - sigma))


def silu(value):
    return value / (1.0 + jnp.exp(-value))


def kernel(
    nz, ny, scale,
    feat_ref, cot_ref, we_ref, wm_ref, ws_ref, wc_ref, wb_ref, wp_ref,
    decoded_ref, genc_ref, gmid_ref, gdec_ref,
    fh, ch, sh, ph, oh, bh,
    fx, cx, sx, px, ox, bx,
    slope, bskip, bsum, midp, joined, benc, dec_acc, enc_acc, mid_acc, dplane,
    a_mine, a_one, a_two, a_whole, b_mine, b_one, b_two, b_whole,
    hsend, hrecv, as1, ar1, as2, ar2, as3, ar3, bs1, br1, bs2, br2, bs3, br3,
):
    gz, gy = lax.axis_index("gz"), lax.axis_index("gy")
    c1, depth, height, width = feat_ref.shape
    half = width // 2
    c2 = bsum.shape[1]
    chigh = height // 2
    grid = (gz, gy, nz, ny)
    fhalo, chalo, shalo, phalo, ohalo, bhalo = [
        Halo(ref, hsend, hrecv, n, grid) for n, ref in enumerate((fh, ch, sh, ph, oh, bh))
    ]
    column = Group(2 * ny, lax.rem(gz, 2) * ny + gy, lambda t: (gz - lax.rem(gz, 2) + t // ny, lax.rem(t, ny)))
    plane = Group(nz // 2, gz // 2, lambda t: (2 * t + lax.rem(gz, 2), gy))

    barrier = pltpu.get_barrier_semaphore()
    away = gz + 2 * lax.rem(gz, 2) - 1
    arrivals = column.size + plane.size - 2
    for b in (-1, 0, 1):
        near = (away >= 0) & (away < nz) & (gy + b >= 0) & (gy + b < ny)
        arrivals = arrivals + jnp.where(near, 1, 0)

        @pl.when(near)
        def _(b=b):
            pl.semaphore_signal(barrier, inc=1, device_id=(away, gy + b), device_id_type=MESH)
    for group in (column, plane):
        for t in group.others():
            pl.semaphore_signal(barrier, inc=1, device_id=group.peer(t), device_id_type=MESH)

    to_cells = rows_to_cells(c1, height)
    for src, dst in ((feat_ref, fh), (cot_ref, ch)):
        for z in range(depth):
            own = src[:, z].astype(F32).reshape(c1 * height, width).astype(BF)
            own = dot(to_cells, own).astype(BF).reshape(height, c1, width)
            dst[1 + z, pl.ds(1, height)] = own

    pl.semaphore_wait(barrier, arrivals)

    fhalo.start()
    chalo.start()
    for halo in (fhalo, chalo, shalo, phalo, ohalo, bhalo):
        halo.clear()
    a_mine[...] = jnp.zeros(a_mine.shape, BF)
    b_mine[...] = jnp.zeros(b_mine.shape, BF)
    joined[...] = jnp.zeros(joined.shape, BF)
    px[...] = jnp.zeros(px.shape, BF)
    dec_acc[...] = jnp.zeros(dec_acc.shape, F32)
    enc_acc[...] = jnp.zeros(enc_acc.shape, F32)
    mid_acc[...] = jnp.zeros(mid_acc.shape, F32)

    def four(src, dst):
        spread = split_four(width)

        def body(z, carry):
            rows = src[z].reshape((height + 2) * c1, width)
            out = dot(rows, spread).astype(BF).reshape(height + 2, c1, 2 * width)
            for j in range(4):
                dst[z, :, j * c1 : (j + 1) * c1, :] = out[:, :, j * half : (j + 1) * half]
            return carry

        lax.fori_loop(0, depth + 2, body, 0)

    fhalo.arrived()
    four(fh, fx)

    def encode(yc, carry):
        pool = jnp.zeros((c1, half), F32)
        for z in range(depth):
            pre = dot(we_ref[...], pair(fx, z, 2 * yc))
            act = silu(pre).astype(BF)
            der = silu_slope(pre)
            for p in range(2):
                cell = act[:, p * half : (p + 1) * half]
                slope[z, 2 * yc + p] = der[:, p * half : (p + 1) * half]
                for q in range(2):
                    part = cell[q * c1 : (q + 1) * c1]
                    sh[1 + z, 1 + 2 * yc + p, :, q * half : (q + 1) * half] = part
                    joined[z, 2 * yc + p, q * 128 + c2 : q * 128 + c2 + c1, :] = part
                    pool = pool + part.astype(F32)
        ph[1, 1 + yc] = (pool * 0.125).astype(BF)
        return carry

    lax.fori_loop(0, chigh, encode, 0)
    phalo.start()
    shalo.start()

    chalo.arrived()
    four(ch, cx)

    def backward(yc, carry):
        low = jnp.zeros((c2, half), F32)
        for z in range(depth):
            out = dot(wb_ref[...], pair(cx, z, 2 * yc))
            for p in range(2):
                for q in range(2):
                    part = out[q * (c1 + c2) : (q + 1) * (c1 + c2), p * half : (p + 1) * half]
                    low = low + part[:c2]
                    bskip[z, 2 * yc + p, q * c1 : (q + 1) * c1, :] = part[c2:]
        bsum[yc] = low
        return carry

    lax.fori_loop(0, chigh, backward, 0)

    sides = shift_both(half)

    def three(src, dst):
        chans = src.shape[2]
        rows = src[...].reshape(src.shape[0] * src.shape[1] * chans, half)
        out = dot(rows, sides).astype(BF).reshape(src.shape[0], src.shape[1], chans, 2 * half)
        dst[:, :, 0:chans, :] = out[..., :half]
        dst[:, :, chans : 2 * chans, :] = src[...]
        dst[:, :, 2 * chans : 3 * chans, :] = out[..., half:]

    phalo.arrived()
    three(ph, px)
    for yc in range(0, chigh, 2):
        pre = dot(wm_ref[...], pair(px, 0, yc))
        for p in range(2):
            cell = pre[:, p * half : (p + 1) * half]
            act = silu(cell).astype(BF)
            oh[1, 1 + yc + p] = act
            for z in range(depth):
                for r in range(2):
                    for q in range(2):
                        joined[z, 2 * (yc + p) + r, q * 128 : q * 128 + c2, :] = act
            bh[1, 1 + yc + p] = (silu_slope(cell) * bsum[yc + p]).astype(BF)
    bhalo.start()
    ohalo.start()

    def decoder_grad(yc, carry):
        for z in range(depth):
            own = jnp.concatenate([joined[z, 2 * yc], joined[z, 2 * yc + 1]], axis=1)
            for w in range(3):
                for v in range(3):
                    field = jnp.concatenate(
                        [cx[z + w, 2 * yc + v], cx[z + w, 2 * yc + 1 + v]], axis=1
                    )
                    dec_acc[3 * w + v] += dot_nt(field, own)
        return carry

    lax.fori_loop(0, chigh, decoder_grad, 0)
    for kk in range(9):
        for kx in range(3):
            a_mine[kk, kx * c1 : (kx + 1) * c1, :] = (
                dec_acc[8 - kk, (2 - kx) * c1 : (3 - kx) * c1, 0:128]
                + dec_acc[8 - kk, (3 - kx) * c1 : (4 - kx) * c1, 128:256]
            ).astype(BF)

    for yc in range(0, chigh, 2):
        own = jnp.concatenate([bh[1, 1 + yc], bh[1, 2 + yc]], axis=1)
        mid_acc[...] += dot_nt(own, pair(px, 0, yc))
    for n in range(18):
        kk, h = n // 2, n % 2
        a_mine[9 + n // 3, (n % 3) * 32 : (n % 3 + 1) * 32, :] = mid_acc[
            h * 32 : (h + 1) * 32, kk * 128 : (kk + 1) * 128
        ].astype(BF)
    a_total = Total(plane, column, a_mine, a_one, a_two, a_whole, (as1, ar1, as2, ar2, as3, ar3))
    a_total.start1()

    bhalo.arrived()
    three(bh, bx)
    for yc in range(0, chigh, 2):
        pool = dot(wp_ref[...], pair(bx, 0, yc)) * 0.125
        for p in range(2):
            up = pool[:, p * half : (p + 1) * half]
            up = jnp.concatenate([up, up], axis=0)
            for z in range(depth):
                for r in range(2):
                    y = 2 * (yc + p) + r
                    benc[z, y] = (slope[z, y] * (bskip[z, y] + up)).astype(BF)

    def encoder_grad(yc, carry):
        for z in range(depth):
            own = jnp.concatenate([benc[z, 2 * yc], benc[z, 2 * yc + 1]], axis=1)
            enc_acc[...] += dot_nt(own, pair(fx, z, 2 * yc))
        return carry

    lax.fori_loop(0, chigh, encoder_grad, 0)
    for kk in range(9):
        even = enc_acc[0:c1, kk * 128 : (kk + 1) * 128]
        odd = enc_acc[c1 : 2 * c1, kk * 128 : (kk + 1) * 128]
        piece = (even + pltpu.roll(odd, 128 - c1, 1)).astype(BF)
        for h in range(2):
            n = 2 * kk + h
            b_mine[n // 3, (n % 3) * 16 : (n % 3 + 1) * 16, :] = piece[h * 16 : (h + 1) * 16]
    b_total = Total(column, plane, b_mine, b_one, b_two, b_whole, (bs1, br1, bs2, br2, bs3, br3))
    b_total.start1()
    a_total.start2()

    shalo.arrived()
    turn = shift_parity(width)

    def four_skip(z, carry):
        rows = sh[z].reshape((height + 2) * c1, width)
        out = dot(rows, turn).astype(BF).reshape(height + 2, c1, width)
        sx[z, :, 0:c1, :] = out[:, :, :half]
        sx[z, :, c1 : 2 * c1, :] = sh[z, :, :, 0:half]
        sx[z, :, 2 * c1 : 3 * c1, :] = sh[z, :, :, half:width]
        sx[z, :, 3 * c1 : 4 * c1, :] = out[:, :, half:]
        return carry

    lax.fori_loop(0, depth + 2, four_skip, 0)
    ohalo.arrived()
    three(oh, ox)
    b_total.start2()
    a_total.start3()

    def decode(yc, carry):
        for z in range(depth):
            out = dot(ws_ref[...], pair(sx, z, 2 * yc))
            for p in range(2):
                field = ox[pl.ds(z, 2), pl.ds(yc + p, 2)].reshape(4 * 3 * c2, half)
                row = (out[:, p * half : (p + 1) * half] + dot(wc_ref[2 * z + p], field)).astype(BF)
                for q in range(2):
                    dplane[z, 2 * yc + p, :, q * half : (q + 1) * half] = row[q * c1 : (q + 1) * c1]
        return carry

    lax.fori_loop(0, chigh, decode, 0)
    to_rows = cells_to_rows(c1, height)
    merge = merge_parity(width)
    for z in range(depth):
        rows = dplane[z].reshape(height * c1, width)
        rows = dot(rows, merge).astype(BF)
        decoded_ref[:, z] = dot(to_rows, rows).reshape(c1, height, width).astype(BF)

    b_total.start3()
    a_total.finish()
    for kk in range(9):
        for kx in range(3):
            gdec_ref[3 * kk + kx] = a_whole[kk, kx * c1 : (kx + 1) * c1, 0 : c1 + c2].astype(F32) * scale
    for n in range(18):
        kk, h = n // 2, n % 2
        piece = a_whole[9 + n // 3, (n % 3) * 32 : (n % 3 + 1) * 32, :].astype(F32) * scale
        for kx in range(3):
            gmid_ref[3 * kk + kx, h * 32 : (h + 1) * 32, :] = piece[:, kx * 32 : (kx + 1) * 32]
    b_total.finish()
    for n in range(18):
        kk, h = n // 2, n % 2
        piece = b_whole[n // 3, (n % 3) * 16 : (n % 3 + 1) * 16, :].astype(F32) * scale
        for kx in range(3):
            genc_ref[3 * kk + kx, h * 16 : (h + 1) * 16, :] = piece[:, kx * 32 : (kx + 1) * 32]

    for halo in (fhalo, chalo, shalo, phalo, ohalo, bhalo):
        halo.sent()
    a_total.drain()
    b_total.drain()


def fine_weights(w):
    outs, ins = w.shape[1:]
    w = w.reshape(9, 3, outs, ins).transpose(2, 0, 1, 3).reshape(outs, 9, 3 * ins)
    even = jnp.pad(w, ((0, 0), (0, 0), (0, ins)))
    odd = jnp.pad(w, ((0, 0), (0, 0), (ins, 0)))
    return jnp.concatenate([even, odd], axis=0).reshape(2 * outs, 9 * 4 * ins)


def coarse_weights(w, slots):
    outs, ins = w.shape[1:]
    w = w.reshape(9, 3, outs, ins).transpose(2, 0, 1, 3).reshape(outs, 9, 3 * ins)
    w = jnp.pad(w, ((0, 0), (0, 0), (0, (slots - 3) * ins)))
    return w.reshape(outs, 9 * slots * ins)


def flipped(w):
    return jnp.flip(w, 0).transpose(0, 2, 1)


def up_weights(w):
    outs, ins = w.shape[1:]
    w = w.astype(F32).reshape(3, 3, 3, outs, ins)

    def two(v, dim):
        a, b, c = (lax.index_in_dim(v, i, dim, keepdims=False) for i in range(3))
        return [[a, b + c], [a + b, c]]

    listed = []
    for z in two(w, 0):
        for y in zip(*[two(v, 0) for v in z]):
            rows = []
            for q in range(2):
                cols = []
                for cz in range(2):
                    for cy in range(2):
                        x = two(y[cz][cy], 0)[q]
                        blank = jnp.zeros_like(x[0])
                        cols += [x[0], x[1], blank] if q == 0 else [blank, x[0], x[1]]
                rows.append(jnp.concatenate(cols, axis=1))
            listed.append(jnp.concatenate(rows, axis=0))
    return jnp.stack(listed).astype(BF)


def local(features, w_enc, w_mid, w_dec, cotangent):
    nz, ny = lax.axis_size("gz"), lax.axis_size("gy")
    c1, depth, height, width = features.shape
    c2 = w_mid.shape[1]
    half, ch = width // 2, height // 2
    assert depth == 2 and c1 == 32 and c2 == 64 and half == 128
    we = fine_weights(w_enc)
    wm = coarse_weights(w_mid, 4)
    ws = fine_weights(w_dec[:, :, c2:])
    wc = up_weights(w_dec[:, :, :c2])
    wb = fine_weights(flipped(w_dec))
    wp = coarse_weights(flipped(w_mid), 3)
    scale = (depth * nz * height * ny * width) ** (-0.5)
    n1, n2 = nz // 2, 2 * ny
    vmem = pl.BlockSpec(memory_space=pltpu.VMEM)
    dma = pltpu.SemaphoreType.DMA
    fine, coarse = (depth + 2, height + 2), (3, ch + 2)
    decoded, genc, gmid, gdec = pl.pallas_call(
        functools.partial(kernel, nz, ny, scale),
        out_shape=(
            jax.ShapeDtypeStruct(features.shape, BF),
            jax.ShapeDtypeStruct(w_enc.shape, F32),
            jax.ShapeDtypeStruct(w_mid.shape, F32),
            jax.ShapeDtypeStruct(w_dec.shape, F32),
        ),
        in_specs=[vmem] * 8,
        out_specs=[vmem] * 4,
        scratch_shapes=[
            pltpu.VMEM(fine + (c1, width), BF),
            pltpu.VMEM(fine + (c1, width), BF),
            pltpu.VMEM(fine + (c1, width), BF),
            pltpu.VMEM(coarse + (c1, half), BF),
            pltpu.VMEM(coarse + (c2, half), BF),
            pltpu.VMEM(coarse + (c2, half), BF),
            pltpu.VMEM(fine + (4 * c1, half), BF),
            pltpu.VMEM(fine + (4 * c1, half), BF),
            pltpu.VMEM(fine + (4 * c1, half), BF),
            pltpu.VMEM(coarse + (4 * c1, half), BF),
            pltpu.VMEM(coarse + (3 * c2, half), BF),
            pltpu.VMEM(coarse + (3 * c2, half), BF),
            pltpu.VMEM((depth, height, 2 * c1, half), F32),
            pltpu.VMEM((depth, height, 2 * c1, half), F32),
            pltpu.VMEM((ch, c2, half), F32),
            pltpu.VMEM((ch, c2, half), F32),
            pltpu.VMEM((depth, height, 256, half), BF),
            pltpu.VMEM((depth, height, 2 * c1, half), BF),
            pltpu.VMEM((9, 4 * c1, 256), F32),
            pltpu.VMEM((2 * c1, 9 * 128), F32),
            pltpu.VMEM((c2, 9 * 128), F32),
            pltpu.VMEM((depth, height, c1, width), BF),
            pltpu.VMEM((n1, 96, 128), BF),
            pltpu.VMEM((n1, 96, 128), BF),
            pltpu.VMEM((n2, 96, 128), BF),
            pltpu.VMEM((n1, 96, 128), BF),
            pltpu.VMEM((n2, 48, 128), BF),
            pltpu.VMEM((n2, 48, 128), BF),
            pltpu.VMEM((n1, 48, 128), BF),
            pltpu.VMEM((n2, 48, 128), BF),
            dma((6, 8)), dma((6, 8)),
            dma((n1,)), dma((n1,)), dma((n2,)), dma((n2,)), dma((n1,)), dma((n1,)),
            dma((n2,)), dma((n2,)), dma((n1,)), dma((n1,)), dma((n2,)), dma((n2,)),
        ],
        compiler_params=pltpu.CompilerParams(
            collective_id=0, has_side_effects=True, vmem_limit_bytes=48 * 2**20
        ),
    )(features, cotangent, we, wm, ws, wc, wb, wp)
    return decoded, genc, gmid, gdec


def solution(mesh):
    placed = (P(None, "gz", "gy", None), P(), P(), P(), P(None, "gz", "gy", None))
    return jax.shard_map(
        local,
        mesh=mesh,
        in_specs=placed,
        out_specs=(P(None, "gz", "gy", None), P(), P(), P()),
        check_vma=False,
    )
```

profile of v0, /device:TPU:1, one launch (start us, length us, event | category | flops | bytes accessed | tf_op | source)
XLA Modules:
  0.0 72.3 jit_solution(6091085021607285570)
XLA Ops:
  0.6 1.0 %rev.9 = bf16[27,64,32]{1,2,0:T(8,128)(2,1)S(1)} reverse(bf16[27,64,32]{1,2,0:T(8,128)(2,1)} %param.7), dimensions={0} | reverse | bytes 221184 | tf_op jit(solution)/shard_map/jit(_flip)/rev | solution.py:479
  1.6 0.2 copy.31
  1.8 0.2 reshape.152.wp_ref
  2.0 0.1 slice.314
  2.2 0.2 copy.32
  2.3 0.2 reshape.146
  2.5 0.0 copy-start.3
  2.5 0.4 copy-done.4
  3.0 0.2 copy.33
  3.1 0.2 reshape.140
  3.3 0.1 copy_bitcast_fusion.3
  3.4 0.1 copy-done.3
  3.5 0.1 pad.28
  3.5 0.2 copy.23.wm_ref
  3.7 0.2 fusion.2
  3.9 0.3 copy.21.wb_ref
  4.6 0.1 concatenate.66
  4.7 0.1 concatenate.65
  4.8 0.1 concatenate.69
  5.0 0.1 concatenate.68
  5.1 0.1 concatenate.63
  5.2 0.1 concatenate.62
  5.4 0.1 concatenate.60
  5.5 0.1 concatenate.59
  5.6 0.1 pad_maximum_fusion.wc_ref
  5.7 0.5 copy-done
  6.2 0.1 copy-done.1
  6.2 62.7 %shard_map.84 = (bf16[32,2,8,256]{3,2,1,0:T(8,128)(2,1)S(1)}, f32[27,32,32]{2,1,0:T(8,128)S(1)}, f32[27,64,32]{2,1,0:T(8,128)S(1)}, f32[27,32,96]{2,1,0:T(8,128)S(1)}) custom-call(bf16[32,2,8,256]{3,2,1,0:T(8,128)(2,1)S(1)} %copy-done, bf16[32,2,8,256]{3,2,1,0:T(8,128)(2,1)S(1)} %copy-done.1, bf16[64,1152]{1,0:T(8,128)(2,1)S(1)} %get-tuple-element.97.we_ref, ...), custom_call_target="tpu_custom_call" | custom-call | tf_op jit(solution)/shard_map/pallas_call | solution.py:523
  69.0 1.1 %copy.22 = f32[27,64,32]{1,2,0:T(8,128)} copy(f32[27,64,32]{2,1,0:T(8,128)S(1)} %get-tuple-element.10) | data formatting | bytes 442368 | tf_op jit(solution)/shard_map/pallas_call | solution.py:523
  70.0 0.7 copy.37
  70.8 0.8 %copy.38 = f32[27,32,32]{2,1,0:T(8,128)} copy(f32[27,32,32]{2,1,0:T(8,128)S(1)} %get-tuple-element.103) | data formatting | bytes 221184
  71.5 0.8 %copy.39 = f32[27,32,96]{2,1,0:T(8,128)} copy(f32[27,32,96]{2,1,0:T(8,128)S(1)} %get-tuple-element.105) | data formatting | bytes 663552
  (33 shorter events, 0.4 us)
Async XLA Ops:
  0.6 1.4 %copy-start.2 = (bf16[27,32,96]{2,1,0:T(8,128)(2,1)S(1)}, bf16[27,32,96]{2,1,0:T(8,128)(2,1)}, u32[]{:S(2)}) copy-start(bf16[27,32,96]{2,1,0:T(8,128)(2,1)} %param.8) | copy-start | bytes 497668
  2.0 0.9 %copy-start.4 = (bf16[27,32,32]{2,1,0:T(8,128)(2,1)S(1)}, bf16[27,32,32]{2,1,0:T(8,128)(2,1)}, u32[]{:S(2)}) copy-start(bf16[27,32,32]{2,1,0:T(8,128)(2,1)} %param.6) | copy-start | bytes 165892
  2.5 1.0 %copy-start.3 = (bf16[27,64,32]{1,2,0:T(8,128)(2,1)S(1)}, bf16[27,64,32]{1,2,0:T(8,128)(2,1)}, u32[]{:S(2)}) copy-start(bf16[27,64,32]{1,2,0:T(8,128)(2,1)} %param.7) | copy-start | bytes 331780
  5.2 1.0 %copy-start = (bf16[32,2,8,256]{3,2,1,0:T(8,128)(2,1)S(1)}, bf16[32,2,8,256]{3,2,1,0:T(8,128)(2,1)}, u32[]{:S(2)}) copy-start(bf16[32,2,8,256]{3,2,1,0:T(8,128)(2,1)} %feat_ref.1) | copy-start | bytes 786436
  5.2 1.0 %copy-start.1 = (bf16[32,2,8,256]{3,2,1,0:T(8,128)(2,1)S(1)}, bf16[32,2,8,256]{3,2,1,0:T(8,128)(2,1)}, u32[]{:S(2)}) copy-start(bf16[32,2,8,256]{3,2,1,0:T(8,128)(2,1)} %cot_ref.1) | copy-start | bytes 786436
where the time goes:
time: 72.5 us; the launch traced here: 72.3 us
  Pallas kernels  62.7 us (86%)
  local copies, waits for them, and re-layouts  7.91 us (11%)
  between operations  1 us (1%)
    pallas_call x1, Pallas kernels, local(): pl.pallas_call(functools.partial(kernel, nz, ny, scale), out_shape=(jax.S...  62.7 us
    unnamed x13, local copies, waits for them, and re-layouts  3.29 us

commit v1 on v0

--- a/solution.py
+++ b/solution.py
@@ -67,6 +67,39 @@
     return hot(s == 2 * (r % half) + r // half)
 
 
+def place(z, y):
+    return (z - lax.rem(z, 2) + y // 2, 2 * lax.rem(y, 2) + lax.rem(z, 2))
+
+
+def block(gz, gy):
+    return gz - lax.rem(gz, 2) + lax.rem(gy, 2), 2 * lax.rem(gz, 2) + gy // 2
+
+
+class Move:
+    def __init__(self, src, dst, send, recv, peer, stays):
+        self.src, self.dst, self.send, self.recv = src, dst, send, recv
+        self.peer, self.stays = peer, stays
+
+    def remote(self):
+        return pltpu.make_async_remote_copy(
+            src_ref=self.src, dst_ref=self.dst, send_sem=self.send, recv_sem=self.recv,
+            device_id=self.peer, device_id_type=MESH,
+        )
+
+    def either(self, near, far):
+        pl.when(self.stays)(lambda: near(pltpu.make_async_copy(self.src, self.dst, self.recv)))
+        pl.when(jnp.logical_not(self.stays))(lambda: far(self.remote()))
+
+    def start(self):
+        self.either(lambda c: c.start(), lambda c: c.start())
+
+    def wait_recv(self):
+        self.either(lambda c: c.wait(), lambda c: c.wait_recv())
+
+    def wait_send(self):
+        pl.when(jnp.logical_not(self.stays))(lambda: self.remote().wait_send())
+
+
 class Halo:
     def __init__(self, ref, send, recv, number, grid):
         self.ref, self.send, self.recv, self.number = ref, send, recv, number
@@ -89,7 +122,7 @@
 
     def copy(self, i):
         a, b = DIRECTIONS[i]
-        peer = (lax.rem(self.gz + a + self.nz, self.nz), lax.rem(self.gy + b + self.ny, self.ny))
+        peer = place(lax.rem(self.gz + a + self.nz, self.nz), lax.rem(self.gy + b + self.ny, self.ny))
         return pltpu.make_async_remote_copy(
             src_ref=self.ref.at[self.source(a, self.depth), self.source(b, self.height)],
             dst_ref=self.ref.at[self.target(a, self.depth), self.target(b, self.height)],
@@ -99,8 +132,8 @@
             device_id_type=MESH,
         )
 
-    def start(self):
-        for i in (1, 6, 3, 4, 0, 2, 5, 7):
+    def start(self, listed=(1, 6, 3, 4, 0, 2, 5, 7)):
+        for i in listed:
             pl.when(self.exists(*DIRECTIONS[i]))(lambda i=i: self.copy(i).start())
 
     def clear(self):
@@ -120,11 +153,11 @@
 
 
 class Group:
-    def __init__(self, size, me, peer):
-        self.size, self.me, self.peer = size, me, peer
+    def __init__(self, size, me, peer, listed):
+        self.size, self.me, self.peer, self.listed = size, me, peer, listed
 
     def others(self):
-        return [lax.rem(self.me + d, self.size) for d in range(1, self.size)]
+        return self.listed
 
 
 class Total:
@@ -207,60 +240,110 @@
 
 def kernel(
     nz, ny, scale,
-    feat_ref, cot_ref, we_ref, wm_ref, ws_ref, wc_ref, wb_ref, wp_ref,
+    feat_ref, cot_ref, wenc_hbm, wmid_hbm, wdec_hbm,
     decoded_ref, genc_ref, gmid_ref, gdec_ref,
     fh, ch, sh, ph, oh, bh,
     fx, cx, sx, px, ox, bx,
-    slope, bskip, bsum, midp, joined, benc, dec_acc, enc_acc, mid_acc, dplane,
+    wenc_ref, wmid_ref, wdec_ref, wsem, we_ref, wm_ref, ws_ref, wc_ref, wb_ref, wp_ref, turned,
+    slope, bskip, bsum, boxed, skips, benc, dec_acc, enc_acc, mid_acc, dplane,
     a_mine, a_one, a_two, a_whole, b_mine, b_one, b_two, b_whole,
-    hsend, hrecv, as1, ar1, as2, ar2, as3, ar3, bs1, br1, bs2, br2, bs3, br3,
+    fin, cin, dout, msend, mrecv, hsend, hrecv, as1, ar1, as2, ar2, as3, ar3, bs1, br1, bs2, br2, bs3, br3,
 ):
     gz, gy = lax.axis_index("gz"), lax.axis_index("gy")
+    vz, vy = block(gz, gy)
+    stays = (vz == gz) & (vy == gy)
     c1, depth, height, width = feat_ref.shape
     half = width // 2
     c2 = bsum.shape[1]
     chigh = height // 2
-    grid = (gz, gy, nz, ny)
+    grid = (vz, vy, nz, ny)
     fhalo, chalo, shalo, phalo, ohalo, bhalo = [
         Halo(ref, hsend, hrecv, n, grid) for n, ref in enumerate((fh, ch, sh, ph, oh, bh))
     ]
-    column = Group(2 * ny, lax.rem(gz, 2) * ny + gy, lambda t: (gz - lax.rem(gz, 2) + t // ny, lax.rem(t, ny)))
-    plane = Group(nz // 2, gz // 2, lambda t: (2 * t + lax.rem(gz, 2), gy))
+    near, core = gz // 2, lax.rem(gy, 2)
+    chip = ny // 2 * lax.rem(gz, 2) + gy // 2
+    column = Group(
+        2 * ny,
+        2 * chip + core,
+        lambda t: (gz - lax.rem(gz, 2) + t // ny, lax.rem(t, ny)),
+        [
+            2 * lax.rem(chip + d, ny) + lax.rem(core + e, 2)
+            for d, e in ((2, 0), (2, 1), (1, 0), (3, 0), (1, 1), (3, 1), (0, 1))
+        ],
+    )
+    side = 4
+    far = {0: 0, 1: 1, 2: 2, 3: 1}
+    steps = sorted(((a, b) for a in range(side) for b in range(side)), key=lambda s: -far[s[0]] - far[s[1]])
+    plane = Group(
+        nz // 2,
+        near,
+        lambda t: (2 * t + lax.rem(gz, 2), gy),
+        [
+            side * lax.rem(near // side + a, side) + lax.rem(lax.rem(near, side) + b, side)
+            for a, b in steps[:-1]
+        ],
+    )
 
     barrier = pltpu.get_barrier_semaphore()
-    away = gz + 2 * lax.rem(gz, 2) - 1
+    away = vz + 2 * lax.rem(vz, 2) - 1
     arrivals = column.size + plane.size - 2
     for b in (-1, 0, 1):
-        near = (away >= 0) & (away < nz) & (gy + b >= 0) & (gy + b < ny)
+        near = (away >= 0) & (away < nz) & (vy + b >= 0) & (vy + b < ny)
         arrivals = arrivals + jnp.where(near, 1, 0)
 
         @pl.when(near)
         def _(b=b):
-            pl.semaphore_signal(barrier, inc=1, device_id=(away, gy + b), device_id_type=MESH)
+            pl.semaphore_signal(barrier, inc=1, device_id=place(away, vy + b), device_id_type=MESH)
     for group in (column, plane):
         for t in group.others():
             pl.semaphore_signal(barrier, inc=1, device_id=group.peer(t), device_id_type=MESH)
 
+    weights = [
+        pltpu.make_async_copy(src, dst, wsem.at[n])
+        for n, (src, dst) in enumerate(
+            ((wenc_hbm, wenc_ref), (wmid_hbm, wmid_ref), (wdec_hbm, wdec_ref))
+        )
+    ]
+    for copy in weights:
+        copy.start()
+    target = place(gz, gy)
+    moves = [
+        [
+            Move(src.at[:, z], dst.at[:, z], msend.at[n, z], mrecv.at[n, z], target, stays)
+            for z in range(depth)
+        ]
+        for n, (src, dst) in enumerate(((feat_ref, fin), (cot_ref, cin)))
+    ]
     to_cells = rows_to_cells(c1, height)
-    for src, dst in ((feat_ref, fh), (cot_ref, ch)):
+
+    def take(n, src, dst, halo):
         for z in range(depth):
+            moves[n][z].wait_recv()
             own = src[:, z].astype(F32).reshape(c1 * height, width).astype(BF)
             own = dot(to_cells, own).astype(BF).reshape(height, c1, width)
             dst[1 + z, pl.ds(1, height)] = own
+            halo.start((1, 0, 2) if z == 0 else (6, 5, 7, 3, 4))
 
     pl.semaphore_wait(barrier, arrivals)
-
-    fhalo.start()
-    chalo.start()
+    for listed in moves:
+        for copy in listed:
+            copy.start()
     for halo in (fhalo, chalo, shalo, phalo, ohalo, bhalo):
         halo.clear()
     a_mine[...] = jnp.zeros(a_mine.shape, BF)
     b_mine[...] = jnp.zeros(b_mine.shape, BF)
-    joined[...] = jnp.zeros(joined.shape, BF)
+    boxed[...] = jnp.zeros(boxed.shape, BF)
+    ox[...] = jnp.zeros(ox.shape, BF)
+    bx[...] = jnp.zeros(bx.shape, BF)
+    for copy in weights:
+        copy.wait()
+    prepare(wenc_ref, wmid_ref, wdec_ref, we_ref, wm_ref, ws_ref, wc_ref, wb_ref, wp_ref, turned)
     px[...] = jnp.zeros(px.shape, BF)
     dec_acc[...] = jnp.zeros(dec_acc.shape, F32)
     enc_acc[...] = jnp.zeros(enc_acc.shape, F32)
     mid_acc[...] = jnp.zeros(mid_acc.shape, F32)
+    take(0, fin, fh, fhalo)
+    take(1, cin, ch, chalo)
 
     def four(src, dst):
         spread = split_four(width)
@@ -289,7 +372,7 @@
                 for q in range(2):
                     part = cell[q * c1 : (q + 1) * c1]
                     sh[1 + z, 1 + 2 * yc + p, :, q * half : (q + 1) * half] = part
-                    joined[z, 2 * yc + p, q * 128 + c2 : q * 128 + c2 + c1, :] = part
+                    skips[z, 2 * yc + p, q * c1 : (q + 1) * c1, :] = part
                     pool = pool + part.astype(F32)
         ph[1, 1 + yc] = (pool * 0.125).astype(BF)
         return carry
@@ -315,6 +398,18 @@
 
     lax.fori_loop(0, chigh, backward, 0)
 
+    def box(yc, carry):
+        for w in range(3):
+            low = cx[w, pl.ds(2 * yc, 4)].astype(F32) + cx[w + 1, pl.ds(2 * yc, 4)].astype(F32)
+            for v in range(3):
+                both = low[v] + low[v + 1]
+                boxed[pl.ds((3 * w + v) * 3 * c1, 3 * c1), pl.ds(pl.multiple_of(yc * half, half), half)] = (
+                    both[: 3 * c1] + both[c1:]
+                ).astype(BF)
+        return carry
+
+    lax.fori_loop(0, chigh, box, 0)
+
     sides = shift_both(half)
 
     def three(src, dst):
@@ -333,43 +428,50 @@
             cell = pre[:, p * half : (p + 1) * half]
             act = silu(cell).astype(BF)
             oh[1, 1 + yc + p] = act
-            for z in range(depth):
-                for r in range(2):
-                    for q in range(2):
-                        joined[z, 2 * (yc + p) + r, q * 128 : q * 128 + c2, :] = act
             bh[1, 1 + yc + p] = (silu_slope(cell) * bsum[yc + p]).astype(BF)
     bhalo.start()
     ohalo.start()
 
+    own = jnp.concatenate([oh[1, 1 + yc] for yc in range(chigh)], axis=1)
+    none = jnp.zeros_like(own)
+    low = dot_nt(boxed[: 14 * c1], jnp.concatenate([own, none], axis=0)) + dot_nt(
+        boxed[14 * c1 :], jnp.concatenate([none, own], axis=0)
+    )
+    a_mine[0:7] = low.astype(BF).reshape(7, 64, 128)
+
+    for yc in range(0, chigh, 2):
+        own = jnp.concatenate([bh[1, 1 + yc], bh[1, 2 + yc]], axis=1)
+        mid_acc[...] += dot_nt(pair(px, 0, yc), jnp.concatenate([own, own], axis=0))
+
+    def mid_rows(k):
+        row = (k // 3) * 128 + (k % 3) * c1
+        return mid_acc[row : row + c1, :]
+
+    first = iota((c1, 128), 1) < c2
+    for d in range(14):
+        piece = jnp.where(first, mid_rows(d), mid_rows(d + 14)) if d < 13 else mid_rows(d)
+        a_mine[7 + d // 2, (d % 2) * 32 : (d % 2 + 1) * 32, :] = piece.astype(BF)
+    a_total = Total(plane, column, a_mine, a_one, a_two, a_whole, (as1, ar1, as2, ar2, as3, ar3))
+    a_total.start1()
+
     def decoder_grad(yc, carry):
         for z in range(depth):
-            own = jnp.concatenate([joined[z, 2 * yc], joined[z, 2 * yc + 1]], axis=1)
-            for w in range(3):
-                for v in range(3):
-                    field = jnp.concatenate(
-                        [cx[z + w, 2 * yc + v], cx[z + w, 2 * yc + 1 + v]], axis=1
-                    )
-                    dec_acc[3 * w + v] += dot_nt(field, own)
+            own = jnp.concatenate([skips[z, 2 * yc], skips[z, 2 * yc + 1]], axis=1)
+            dec_acc[...] += dot_nt(own, pair(cx, z, 2 * yc))
         return carry
 
     lax.fori_loop(0, chigh, decoder_grad, 0)
-    for kk in range(9):
-        for kx in range(3):
-            a_mine[kk, kx * c1 : (kx + 1) * c1, :] = (
-                dec_acc[8 - kk, (2 - kx) * c1 : (3 - kx) * c1, 0:128]
-                + dec_acc[8 - kk, (3 - kx) * c1 : (4 - kx) * c1, 128:256]
-            ).astype(BF)
-
-    for yc in range(0, chigh, 2):
-        own = jnp.concatenate([bh[1, 1 + yc], bh[1, 2 + yc]], axis=1)
-        mid_acc[...] += dot_nt(own, pair(px, 0, yc))
-    for n in range(18):
-        kk, h = n // 2, n % 2
-        a_mine[9 + n // 3, (n % 3) * 32 : (n % 3 + 1) * 32, :] = mid_acc[
-            h * 32 : (h + 1) * 32, kk * 128 : (kk + 1) * 128
-        ].astype(BF)
-    a_total = Total(plane, column, a_mine, a_one, a_two, a_whole, (as1, ar1, as2, ar2, as3, ar3))
-    a_total.start1()
+
+    def pack(acc, first):
+        for kk in range(9):
+            even = acc[0:c1, kk * 128 : (kk + 1) * 128]
+            odd = acc[c1 : 2 * c1, kk * 128 : (kk + 1) * 128]
+            piece = (even + pltpu.roll(odd, 128 - c1, 1)).astype(BF)
+            for h in range(2):
+                n = first + 2 * kk + h
+                b_mine[n // 5, (n % 5) * 16 : (n % 5 + 1) * 16, :] = piece[h * 16 : (h + 1) * 16]
+
+    pack(dec_acc, 18)
 
     bhalo.arrived()
     three(bh, bx)
@@ -390,13 +492,7 @@
         return carry
 
     lax.fori_loop(0, chigh, encoder_grad, 0)
-    for kk in range(9):
-        even = enc_acc[0:c1, kk * 128 : (kk + 1) * 128]
-        odd = enc_acc[c1 : 2 * c1, kk * 128 : (kk + 1) * 128]
-        piece = (even + pltpu.roll(odd, 128 - c1, 1)).astype(BF)
-        for h in range(2):
-            n = 2 * kk + h
-            b_mine[n // 3, (n % 3) * 16 : (n % 3 + 1) * 16, :] = piece[h * 16 : (h + 1) * 16]
+    pack(enc_acc, 0)
     b_total = Total(column, plane, b_mine, b_one, b_two, b_whole, (bs1, br1, bs2, br2, bs3, br3))
     b_total.start1()
     a_total.start2()
@@ -423,7 +519,7 @@
         for z in range(depth):
             out = dot(ws_ref[...], pair(sx, z, 2 * yc))
             for p in range(2):
-                field = ox[pl.ds(z, 2), pl.ds(yc + p, 2)].reshape(4 * 3 * c2, half)
+                field = ox[pl.ds(z, 2), pl.ds(yc + p, 2)].reshape(4 * 4 * c2, half)
                 row = (out[:, p * half : (p + 1) * half] + dot(wc_ref[2 * z + p], field)).astype(BF)
                 for q in range(2):
                     dplane[z, 2 * yc + p, :, q * half : (q + 1) * half] = row[q * c1 : (q + 1) * c1]
@@ -432,92 +528,137 @@
     lax.fori_loop(0, chigh, decode, 0)
     to_rows = cells_to_rows(c1, height)
     merge = merge_parity(width)
+    back = [
+        Move(dout.at[:, z], decoded_ref.at[:, z], msend.at[2, z], mrecv.at[2, z], (vz, vy), stays)
+        for z in range(depth)
+    ]
     for z in range(depth):
         rows = dplane[z].reshape(height * c1, width)
         rows = dot(rows, merge).astype(BF)
-        decoded_ref[:, z] = dot(to_rows, rows).reshape(c1, height, width).astype(BF)
+        dout[:, z] = dot(to_rows, rows).reshape(c1, height, width).astype(BF)
+        back[z].start()
 
     b_total.start3()
     a_total.finish()
-    for kk in range(9):
-        for kx in range(3):
-            gdec_ref[3 * kk + kx] = a_whole[kk, kx * c1 : (kx + 1) * c1, 0 : c1 + c2].astype(F32) * scale
+    for r in range(27):
+        half_of, n = r // 14, r % 14
+        gdec_ref[26 - r, :, 0:c2] = a_whole[
+            n // 2, (n % 2) * 32 : (n % 2 + 1) * 32, half_of * c2 : (half_of + 1) * c2
+        ].astype(F32) * scale
+    for k in range(27):
+        half_of, n = k // 14, k % 14
+        gmid_ref[k] = a_whole[
+            7 + n // 2, (n % 2) * 32 : (n % 2 + 1) * 32, half_of * c2 : (half_of + 1) * c2
+        ].astype(F32) * scale
+    b_total.finish()
+
+    def unpack(n):
+        return b_whole[n // 5, (n % 5) * 16 : (n % 5 + 1) * 16, :].astype(F32) * scale
+
     for n in range(18):
         kk, h = n // 2, n % 2
-        piece = a_whole[9 + n // 3, (n % 3) * 32 : (n % 3 + 1) * 32, :].astype(F32) * scale
-        for kx in range(3):
-            gmid_ref[3 * kk + kx, h * 32 : (h + 1) * 32, :] = piece[:, kx * 32 : (kx + 1) * 32]
-    b_total.finish()
-    for n in range(18):
-        kk, h = n // 2, n % 2
-        piece = b_whole[n // 3, (n % 3) * 16 : (n % 3 + 1) * 16, :].astype(F32) * scale
+        piece = unpack(n)
         for kx in range(3):
             genc_ref[3 * kk + kx, h * 16 : (h + 1) * 16, :] = piece[:, kx * 32 : (kx + 1) * 32]
-
+    for kk in range(9):
+        piece = jnp.concatenate([unpack(18 + 2 * kk), unpack(19 + 2 * kk)], axis=0).T
+        for kx in range(3):
+            gdec_ref[3 * (8 - kk) + 2 - kx, :, c2 : c2 + c1] = piece[kx * c1 : (kx + 1) * c1]
+
+    for copy in back:
+        copy.wait_recv()
+    for copy in moves[0] + moves[1] + back:
+        copy.wait_send()
     for halo in (fhalo, chalo, shalo, phalo, ohalo, bhalo):
         halo.sent()
     a_total.drain()
     b_total.drain()
 
 
-def fine_weights(w):
-    outs, ins = w.shape[1:]
-    w = w.reshape(9, 3, outs, ins).transpose(2, 0, 1, 3).reshape(outs, 9, 3 * ins)
-    even = jnp.pad(w, ((0, 0), (0, 0), (0, ins)))
-    odd = jnp.pad(w, ((0, 0), (0, 0), (ins, 0)))
-    return jnp.concatenate([even, odd], axis=0).reshape(2 * outs, 9 * 4 * ins)
-
-
-def coarse_weights(w, slots):
-    outs, ins = w.shape[1:]
-    w = w.reshape(9, 3, outs, ins).transpose(2, 0, 1, 3).reshape(outs, 9, 3 * ins)
-    w = jnp.pad(w, ((0, 0), (0, 0), (0, (slots - 3) * ins)))
-    return w.reshape(outs, 9 * slots * ins)
-
-
-def flipped(w):
-    return jnp.flip(w, 0).transpose(0, 2, 1)
-
-
-def up_weights(w):
-    outs, ins = w.shape[1:]
-    w = w.astype(F32).reshape(3, 3, 3, outs, ins)
-
-    def two(v, dim):
-        a, b, c = (lax.index_in_dim(v, i, dim, keepdims=False) for i in range(3))
-        return [[a, b + c], [a + b, c]]
-
-    listed = []
-    for z in two(w, 0):
-        for y in zip(*[two(v, 0) for v in z]):
-            rows = []
-            for q in range(2):
-                cols = []
-                for cz in range(2):
-                    for cy in range(2):
-                        x = two(y[cz][cy], 0)[q]
-                        blank = jnp.zeros_like(x[0])
-                        cols += [x[0], x[1], blank] if q == 0 else [blank, x[0], x[1]]
-                rows.append(jnp.concatenate(cols, axis=1))
-            listed.append(jnp.concatenate(rows, axis=0))
-    return jnp.stack(listed).astype(BF)
+def split_weights(w_ref, kx):
+    return jnp.concatenate([w_ref[3 * kk + kx] for kk in range(9)], axis=0)
+
+
+def fine_weights(w_ref, first, dst):
+    outs, ins, n = w_ref.shape[1], w_ref.shape[2], dst.shape[1] // 36
+    total = jnp.zeros((9 * outs, 8 * n), F32)
+    for kx in range(3):
+        r, c = iota((ins, 8 * n), 0), iota((ins, 8 * n), 1)
+        px, jx, i = c // (4 * n), (c // n) % 4, c % n
+        total = total + dot(split_weights(w_ref, kx), hot((jx == kx + px) & (r == first + i)))
+    total = total.astype(BF)
+    for kk in range(9):
+        for p in range(2):
+            dst[p * outs : (p + 1) * outs, kk * 4 * n : (kk + 1) * 4 * n] = total[
+                kk * outs : (kk + 1) * outs, p * 4 * n : (p + 1) * 4 * n
+            ]
+
+
+def prepare(wenc_ref, wmid_ref, wdec_ref, we_ref, wm_ref, ws_ref, wc_ref, wb_ref, wp_ref, turned):
+    c1, c2 = wmid_ref.shape[1:]
+    fine_weights(wenc_ref, 0, we_ref)
+    fine_weights(wdec_ref, c2, ws_ref)
+
+    blank = jnp.zeros((c1, c2), BF)
+    rows = [wmid_ref[3 * kk + kx] if kx < 3 else blank for kk in range(9) for kx in range(4)]
+    pick = hot(iota((c2, c2), 0) == iota((c2, c2), 1))
+    wm_ref[...] = dot_nt(pick, jnp.concatenate(rows, axis=0)).astype(BF)
+    total = jnp.zeros((9 * c1, 4 * c2), F32)
+    for kx in range(3):
+        rows = jnp.concatenate([wmid_ref[26 - 3 * kk - kx] for kk in range(9)], axis=0)
+        r, c = iota((c2, 4 * c2), 0), iota((c2, 4 * c2), 1)
+        total = total + dot(rows, hot(c == kx * c2 + r))
+    total = total.astype(BF)
+    for kk in range(9):
+        wp_ref[:, kk * 4 * c2 : (kk + 1) * 4 * c2] = total[kk * c1 : (kk + 1) * c1]
+
+    total = jnp.zeros((9 * c1, 8 * c2), F32)
+    for kx in range(3):
+        r, c = iota((c1 + c2, 8 * c2), 0), iota((c1 + c2, 8 * c2), 1)
+        px, slot, i = c // (4 * c2), (c // c2) % 4, c % c2
+        wanted = (kx + px + 1) // 2
+        total = total + dot(split_weights(wdec_ref, kx), hot((slot == wanted) & (r == i)))
+    parts = [[[0], [1, 2]], [[0, 1], [2]]]
+    for pz in range(2):
+        for py in range(2):
+            for cz in range(2):
+                for cy in range(2):
+                    part = sum(
+                        total[(3 * kz + ky) * c1 : (3 * kz + ky + 1) * c1]
+                        for kz in parts[pz][cz]
+                        for ky in parts[py][cy]
+                    ).astype(BF)
+                    at = (2 * cz + cy) * 4 * c2
+                    for p in range(2):
+                        wc_ref[2 * pz + py, p * c1 : (p + 1) * c1, at : at + 4 * c2] = part[
+                            :, p * 4 * c2 : (p + 1) * 4 * c2
+                        ]
+
+    turned[...] = jnp.zeros(turned.shape, BF)
+    blank = jnp.zeros((c1, c1 + c2), BF)
+    for kk in range(9):
+        for p in range(2):
+            for jx in range(4):
+                kx = jx - p
+                value = wdec_ref[26 - 3 * kk - kx] if 0 <= kx < 3 else blank
+                row = kk * 4 * c1 + jx * c1
+                turned[row : row + c1, p * 128 : p * 128 + c1 + c2] = value
+    r, c = iota((2 * (c1 + c2), 256), 0), iota((2 * (c1 + c2), 256), 1)
+    pick = hot(c == (r // (c1 + c2)) * 128 + r % (c1 + c2))
+    wb_ref[...] = dot_nt(pick, turned[...]).astype(BF)
 
 
 def local(features, w_enc, w_mid, w_dec, cotangent):
     nz, ny = lax.axis_size("gz"), lax.axis_size("gy")
     c1, depth, height, width = features.shape
     c2 = w_mid.shape[1]
+    w_mid = w_mid.transpose(0, 2, 1)
     half, ch = width // 2, height // 2
-    assert depth == 2 and c1 == 32 and c2 == 64 and half == 128
-    we = fine_weights(w_enc)
-    wm = coarse_weights(w_mid, 4)
-    ws = fine_weights(w_dec[:, :, c2:])
-    wc = up_weights(w_dec[:, :, :c2])
-    wb = fine_weights(flipped(w_dec))
-    wp = coarse_weights(flipped(w_mid), 3)
+    assert nz == 32 and ny == 4 and depth == 2 and c1 == 32 and c2 == 64 and half == 128
     scale = (depth * nz * height * ny * width) ** (-0.5)
     n1, n2 = nz // 2, 2 * ny
     vmem = pl.BlockSpec(memory_space=pltpu.VMEM)
+    anywhere = pl.BlockSpec(memory_space=pl.ANY)
     dma = pltpu.SemaphoreType.DMA
     fine, coarse = (depth + 2, height + 2), (3, ch + 2)
     decoded, genc, gmid, gdec = pl.pallas_call(
@@ -528,8 +669,8 @@
             jax.ShapeDtypeStruct(w_mid.shape, F32),
             jax.ShapeDtypeStruct(w_dec.shape, F32),
         ),
-        in_specs=[vmem] * 8,
-        out_specs=[vmem] * 4,
+        in_specs=[anywhere] * 5,
+        out_specs=[anywhere] + [vmem] * 3,
         scratch_shapes=[
             pltpu.VMEM(fine + (c1, width), BF),
             pltpu.VMEM(fine + (c1, width), BF),
@@ -541,35 +682,49 @@
             pltpu.VMEM(fine + (4 * c1, half), BF),
             pltpu.VMEM(fine + (4 * c1, half), BF),
             pltpu.VMEM(coarse + (4 * c1, half), BF),
-            pltpu.VMEM(coarse + (3 * c2, half), BF),
-            pltpu.VMEM(coarse + (3 * c2, half), BF),
+            pltpu.VMEM(coarse + (4 * c2, half), BF),
+            pltpu.VMEM(coarse + (4 * c2, half), BF),
+            pltpu.VMEM(w_enc.shape, BF),
+            pltpu.VMEM(w_mid.shape, BF),
+            pltpu.VMEM(w_dec.shape, BF),
+            dma((3,)),
+            pltpu.VMEM((2 * c1, 36 * c1), BF),
+            pltpu.VMEM((c2, 36 * c1), BF),
+            pltpu.VMEM((2 * c1, 36 * c1), BF),
+            pltpu.VMEM((4, 2 * c1, 16 * c2), BF),
+            pltpu.VMEM((2 * (c1 + c2), 36 * c1), BF),
+            pltpu.VMEM((c1, 36 * c2), BF),
+            pltpu.VMEM((36 * c1, 256), BF),
             pltpu.VMEM((depth, height, 2 * c1, half), F32),
             pltpu.VMEM((depth, height, 2 * c1, half), F32),
             pltpu.VMEM((ch, c2, half), F32),
-            pltpu.VMEM((ch, c2, half), F32),
-            pltpu.VMEM((depth, height, 256, half), BF),
+            pltpu.VMEM((28 * c1, ch * half), BF),
             pltpu.VMEM((depth, height, 2 * c1, half), BF),
-            pltpu.VMEM((9, 4 * c1, 256), F32),
+            pltpu.VMEM((depth, height, 2 * c1, half), BF),
             pltpu.VMEM((2 * c1, 9 * 128), F32),
-            pltpu.VMEM((c2, 9 * 128), F32),
+            pltpu.VMEM((2 * c1, 9 * 128), F32),
+            pltpu.VMEM((9 * 128, 128), F32),
             pltpu.VMEM((depth, height, c1, width), BF),
-            pltpu.VMEM((n1, 96, 128), BF),
-            pltpu.VMEM((n1, 96, 128), BF),
-            pltpu.VMEM((n2, 96, 128), BF),
-            pltpu.VMEM((n1, 96, 128), BF),
-            pltpu.VMEM((n2, 48, 128), BF),
-            pltpu.VMEM((n2, 48, 128), BF),
-            pltpu.VMEM((n1, 48, 128), BF),
-            pltpu.VMEM((n2, 48, 128), BF),
-            dma((6, 8)), dma((6, 8)),
+            pltpu.VMEM((n1, 64, 128), BF),
+            pltpu.VMEM((n1, 64, 128), BF),
+            pltpu.VMEM((n2, 64, 128), BF),
+            pltpu.VMEM((n1, 64, 128), BF),
+            pltpu.VMEM((n2, 80, 128), BF),
+            pltpu.VMEM((n2, 80, 128), BF),
+            pltpu.VMEM((n1, 80, 128), BF),
+            pltpu.VMEM((n2, 80, 128), BF),
+            pltpu.VMEM(features.shape, BF),
+            pltpu.VMEM(features.shape, BF),
+            pltpu.VMEM(features.shape, BF),
+            dma((3, 2)), dma((3, 2)), dma((6, 8)), dma((6, 8)),
             dma((n1,)), dma((n1,)), dma((n2,)), dma((n2,)), dma((n1,)), dma((n1,)),
             dma((n2,)), dma((n2,)), dma((n1,)), dma((n1,)), dma((n2,)), dma((n2,)),
         ],
         compiler_params=pltpu.CompilerParams(
-            collective_id=0, has_side_effects=True, vmem_limit_bytes=48 * 2**20
+            collective_id=0, has_side_effects=True, vmem_limit_bytes=60 * 2**20
         ),
-    )(features, cotangent, we, wm, ws, wc, wb, wp)
-    return decoded, genc, gmid, gdec
+    )(features, cotangent, w_enc, w_mid, w_dec)
+    return decoded, genc, gmid.transpose(0, 2, 1), gdec
 
 
 def solution(mesh):

time: 72.5 us -> 60.7 us (0.84)
  the two profiles are of different devices: /device:TPU:1 before, /device:TPU:41 now
where the time goes in v1:
time: 60.7 us; the launch traced here: 60.4 us
  Pallas kernels  54.9 us (90%)
  local copies, waits for them, and re-layouts  4.83 us (8%)
  between operations  0.65 us (1%)
    pallas_call x1, Pallas kernels, local(): pl.pallas_call(functools.partial(kernel, nz, ny, scale), out_shape=(jax.S...  54.9 us
    unnamed x10, local copies, waits for them, and re-layouts  4.83 us

profile of v1, /device:TPU:41, one launch (start us, length us, event | category | flops | bytes accessed | tf_op | source)
XLA Modules:
  0.0 60.4 jit_solution(15257683275420430638)
XLA Ops:
  0.6 54.9 %shard_map.84 = (bf16[32,2,8,256]{3,2,1,0:T(8,128)(2,1)}, f32[27,32,32]{2,1,0:T(8,128)}, f32[27,32,64]{2,1,0:T(8,128)}, f32[27,32,96]{2,1,0:T(8,128)}) custom-call(bf16[32,2,8,256]{3,2,1,0:T(8,128)(2,1)} %feat_ref.1, bf16[32,2,8,256]{3,2,1,0:T(8,128)(2,1)} %cot_ref.1, bf16[27,32,32]{2,1,0:T(8,128)(2,1)} %wenc_hbm.1, bf16[27,32,64]{2,1,0:T(8,128)(2,1)} %bitcast.3, ...), custom_call_target="tpu_custom_call" | custom-call | tf_op jit(solution)/shard_map/pallas_call | solution.py:664
  55.6 0.0 copy-start.2
  55.6 1.7 %copy.13 = bf16[32,2,8,256]{3,2,1,0:T(8,128)(2,1)} copy(bf16[32,2,8,256]{3,2,1,0:T(8,128)(2,1)} %get-tuple-element.16) | data formatting | bytes 524288
  57.3 0.0 copy-done.2
  57.3 0.0 copy-start.1
  57.3 0.8 %copy.14 = f32[27,32,32]{2,1,0:T(8,128)} copy(f32[27,32,32]{2,1,0:T(8,128)S(1)} %copy-done.2) | data formatting | bytes 221184
  58.1 0.4 copy-done.1
  58.5 0.0 copy-start
  58.5 0.8 %copy.15 = f32[27,64,32]{1,2,0:T(8,128)} copy(f32[27,64,32]{1,2,0:T(8,128)S(1)} %bitcast.2) | data formatting | bytes 442368
  59.3 0.4 copy-done
  59.7 0.8 %copy.16 = f32[27,32,96]{2,1,0:T(8,128)} copy(f32[27,32,96]{2,1,0:T(8,128)S(1)} %copy-done) | data formatting | bytes 663552
Async XLA Ops:
  55.6 1.7 %copy-start.2 = (f32[27,32,32]{2,1,0:T(8,128)S(1)}, f32[27,32,32]{2,1,0:T(8,128)}, u32[]{:S(2)}) copy-start(f32[27,32,32]{2,1,0:T(8,128)} %get-tuple-element.17) | copy-start | bytes 331780
  57.3 1.2 %copy-start.1 = (f32[27,32,64]{2,1,0:T(8,128)S(1)}, f32[27,32,64]{2,1,0:T(8,128)}, u32[]{:S(2)}) copy-start(f32[27,32,64]{2,1,0:T(8,128)} %get-tuple-element.10) | copy-start | bytes 663556
  58.5 1.2 %copy-start = (f32[27,32,96]{2,1,0:T(8,128)S(1)}, f32[27,32,96]{2,1,0:T(8,128)}, u32[]{:S(2)}) copy-start(f32[27,32,96]{2,1,0:T(8,128)} %get-tuple-element.19) | copy-start | bytes 995332

commit v2 on v1

--- a/solution.py
+++ b/solution.py
@@ -239,14 +239,14 @@
 
 
 def kernel(
-    nz, ny, scale,
+    nz, ny,
     feat_ref, cot_ref, wenc_hbm, wmid_hbm, wdec_hbm,
-    decoded_ref, genc_ref, gmid_ref, gdec_ref,
+    decoded_ref, a_whole, b_whole,
     fh, ch, sh, ph, oh, bh,
     fx, cx, sx, px, ox, bx,
     wenc_ref, wmid_ref, wdec_ref, wsem, we_ref, wm_ref, ws_ref, wc_ref, wb_ref, wp_ref, turned,
     slope, bskip, bsum, boxed, skips, benc, dec_acc, enc_acc, mid_acc, dplane,
-    a_mine, a_one, a_two, a_whole, b_mine, b_one, b_two, b_whole,
+    a_mine, a_one, a_two, b_mine, b_one, b_two,
     fin, cin, dout, msend, mrecv, hsend, hrecv, as1, ar1, as2, ar2, as3, ar3, bs1, br1, bs2, br2, bs3, br3,
 ):
     gz, gy = lax.axis_index("gz"), lax.axis_index("gy")
@@ -410,6 +410,28 @@
 
     lax.fori_loop(0, chigh, box, 0)
 
+    def store(dst, n, piece):
+        each = dst.shape[1] // 16
+        dst[n // each, (n % each) * 16 : (n % each + 1) * 16, :] = piece
+
+    def decoder_grad(yc, carry):
+        for z in range(depth):
+            own = jnp.concatenate([skips[z, 2 * yc], skips[z, 2 * yc + 1]], axis=1)
+            dec_acc[...] += dot_nt(own, pair(cx, z, 2 * yc))
+        return carry
+
+    lax.fori_loop(0, chigh, decoder_grad, 0)
+
+    def pack(acc, dst, first):
+        for kk in range(9):
+            even = acc[0:c1, kk * 128 : (kk + 1) * 128]
+            odd = acc[c1 : 2 * c1, kk * 128 : (kk + 1) * 128]
+            piece = (even + pltpu.roll(odd, 128 - c1, 1)).astype(BF)
+            for h in range(2):
+                store(dst, first + 2 * kk + h, piece[h * 16 : (h + 1) * 16])
+
+    pack(dec_acc, a_mine, 56)
+
     sides = shift_both(half)
 
     def three(src, dst):
@@ -437,7 +459,9 @@
     low = dot_nt(boxed[: 14 * c1], jnp.concatenate([own, none], axis=0)) + dot_nt(
         boxed[14 * c1 :], jnp.concatenate([none, own], axis=0)
     )
-    a_mine[0:7] = low.astype(BF).reshape(7, 64, 128)
+    low = low.astype(BF)
+    for n in range(28):
+        store(a_mine, n, low[n * 16 : (n + 1) * 16])
 
     for yc in range(0, chigh, 2):
         own = jnp.concatenate([bh[1, 1 + yc], bh[1, 2 + yc]], axis=1)
@@ -450,28 +474,11 @@
     first = iota((c1, 128), 1) < c2
     for d in range(14):
         piece = jnp.where(first, mid_rows(d), mid_rows(d + 14)) if d < 13 else mid_rows(d)
-        a_mine[7 + d // 2, (d % 2) * 32 : (d % 2 + 1) * 32, :] = piece.astype(BF)
+        piece = piece.astype(BF)
+        for h in range(2):
+            store(a_mine, 28 + 2 * d + h, piece[h * 16 : (h + 1) * 16])
     a_total = Total(plane, column, a_mine, a_one, a_two, a_whole, (as1, ar1, as2, ar2, as3, ar3))
     a_total.start1()
-
-    def decoder_grad(yc, carry):
-        for z in range(depth):
-            own = jnp.concatenate([skips[z, 2 * yc], skips[z, 2 * yc + 1]], axis=1)
-            dec_acc[...] += dot_nt(own, pair(cx, z, 2 * yc))
-        return carry
-
-    lax.fori_loop(0, chigh, decoder_grad, 0)
-
-    def pack(acc, first):
-        for kk in range(9):
-            even = acc[0:c1, kk * 128 : (kk + 1) * 128]
-            odd = acc[c1 : 2 * c1, kk * 128 : (kk + 1) * 128]
-            piece = (even + pltpu.roll(odd, 128 - c1, 1)).astype(BF)
-            for h in range(2):
-                n = first + 2 * kk + h
-                b_mine[n // 5, (n % 5) * 16 : (n % 5 + 1) * 16, :] = piece[h * 16 : (h + 1) * 16]
-
-    pack(dec_acc, 18)
 
     bhalo.arrived()
     three(bh, bx)
@@ -492,7 +499,7 @@
         return carry
 
     lax.fori_loop(0, chigh, encoder_grad, 0)
-    pack(enc_acc, 0)
+    pack(enc_acc, b_mine, 0)
     b_total = Total(column, plane, b_mine, b_one, b_two, b_whole, (bs1, br1, bs2, br2, bs3, br3))
     b_total.start1()
     a_total.start2()
@@ -540,31 +547,7 @@
 
     b_total.start3()
     a_total.finish()
-    for r in range(27):
-        half_of, n = r // 14, r % 14
-        gdec_ref[26 - r, :, 0:c2] = a_whole[
-            n // 2, (n % 2) * 32 : (n % 2 + 1) * 32, half_of * c2 : (half_of + 1) * c2
-        ].astype(F32) * scale
-    for k in range(27):
-        half_of, n = k // 14, k % 14
-        gmid_ref[k] = a_whole[
-            7 + n // 2, (n % 2) * 32 : (n % 2 + 1) * 32, half_of * c2 : (half_of + 1) * c2
-        ].astype(F32) * scale
     b_total.finish()
-
-    def unpack(n):
-        return b_whole[n // 5, (n % 5) * 16 : (n % 5 + 1) * 16, :].astype(F32) * scale
-
-    for n in range(18):
-        kk, h = n // 2, n % 2
-        piece = unpack(n)
-        for kx in range(3):
-            genc_ref[3 * kk + kx, h * 16 : (h + 1) * 16, :] = piece[:, kx * 32 : (kx + 1) * 32]
-    for kk in range(9):
-        piece = jnp.concatenate([unpack(18 + 2 * kk), unpack(19 + 2 * kk)], axis=0).T
-        for kx in range(3):
-            gdec_ref[3 * (8 - kk) + 2 - kx, :, c2 : c2 + c1] = piece[kx * c1 : (kx + 1) * c1]
-
     for copy in back:
         copy.wait_recv()
     for copy in moves[0] + moves[1] + back:
@@ -573,6 +556,42 @@
         halo.sent()
     a_total.drain()
     b_total.drain()
+
+
+def results(
+    scale, moved_hbm, a_hbm, b_hbm, decoded_ref, genc_ref, gmid_ref, gdec_ref, moved_ref, a_ref, b_ref, sem
+):
+    copies = [
+        pltpu.make_async_copy(src, dst, sem.at[n])
+        for n, (src, dst) in enumerate(((a_hbm, a_ref), (b_hbm, b_ref), (moved_hbm, moved_ref)))
+    ]
+    for copy in copies:
+        copy.start()
+    c1, c2 = genc_ref.shape[1], gmid_ref.shape[2]
+
+    def load(src, n):
+        each = src.shape[1] // 16
+        return src[n // each, (n % each) * 16 : (n % each + 1) * 16, :].astype(F32) * scale
+
+    def both(src, n):
+        return jnp.concatenate([load(src, n), load(src, n + 1)], axis=0)
+
+    copies[2].wait()
+    out = pltpu.make_async_copy(moved_ref, decoded_ref, sem.at[3])
+    out.start()
+    copies[0].wait()
+    copies[1].wait()
+    for d in range(14):
+        low, mid = both(a_ref, 2 * d), both(a_ref, 28 + 2 * d)
+        for h in range(2 if d < 13 else 1):
+            gdec_ref[26 - d - 14 * h, :, 0:c2] = low[:, h * c2 : (h + 1) * c2]
+            gmid_ref[d + 14 * h] = mid[:, h * c2 : (h + 1) * c2]
+    for kk in range(9):
+        skip, enc = both(a_ref, 56 + 2 * kk).T, both(b_ref, 2 * kk)
+        for kx in range(3):
+            gdec_ref[3 * (8 - kk) + 2 - kx, :, c2 : c2 + c1] = skip[kx * c1 : (kx + 1) * c1]
+            genc_ref[3 * kk + kx] = enc[:, kx * c1 : (kx + 1) * c1]
+    out.wait()
 
 
 def split_weights(w_ref, kx):
@@ -661,16 +680,15 @@
     anywhere = pl.BlockSpec(memory_space=pl.ANY)
     dma = pltpu.SemaphoreType.DMA
     fine, coarse = (depth + 2, height + 2), (3, ch + 2)
-    decoded, genc, gmid, gdec = pl.pallas_call(
-        functools.partial(kernel, nz, ny, scale),
+    moved, a_sum, b_sum = pl.pallas_call(
+        functools.partial(kernel, nz, ny),
         out_shape=(
             jax.ShapeDtypeStruct(features.shape, BF),
-            jax.ShapeDtypeStruct(w_enc.shape, F32),
-            jax.ShapeDtypeStruct(w_mid.shape, F32),
-            jax.ShapeDtypeStruct(w_dec.shape, F32),
+            jax.ShapeDtypeStruct((n1, 80, 128), BF),
+            jax.ShapeDtypeStruct((n2, 48, 128), BF),
         ),
         in_specs=[anywhere] * 5,
-        out_specs=[anywhere] + [vmem] * 3,
+        out_specs=[anywhere] + [vmem] * 2,
         scratch_shapes=[
             pltpu.VMEM(fine + (c1, width), BF),
             pltpu.VMEM(fine + (c1, width), BF),
@@ -705,14 +723,12 @@
             pltpu.VMEM((2 * c1, 9 * 128), F32),
             pltpu.VMEM((9 * 128, 128), F32),
             pltpu.VMEM((depth, height, c1, width), BF),
-            pltpu.VMEM((n1, 64, 128), BF),
-            pltpu.VMEM((n1, 64, 128), BF),
-            pltpu.VMEM((n2, 64, 128), BF),
-            pltpu.VMEM((n1, 64, 128), BF),
-            pltpu.VMEM((n2, 80, 128), BF),
-            pltpu.VMEM((n2, 80, 128), BF),
+            pltpu.VMEM((n1, 80, 128), BF),
             pltpu.VMEM((n1, 80, 128), BF),
             pltpu.VMEM((n2, 80, 128), BF),
+            pltpu.VMEM((n2, 48, 128), BF),
+            pltpu.VMEM((n2, 48, 128), BF),
+            pltpu.VMEM((n1, 48, 128), BF),
             pltpu.VMEM(features.shape, BF),
             pltpu.VMEM(features.shape, BF),
             pltpu.VMEM(features.shape, BF),
@@ -724,6 +740,24 @@
             collective_id=0, has_side_effects=True, vmem_limit_bytes=60 * 2**20
         ),
     )(features, cotangent, w_enc, w_mid, w_dec)
+    decoded, genc, gmid, gdec = pl.pallas_call(
+        functools.partial(results, scale),
+        out_shape=(
+            jax.ShapeDtypeStruct(features.shape, BF),
+            jax.ShapeDtypeStruct(w_enc.shape, F32),
+            jax.ShapeDtypeStruct(w_mid.shape, F32),
+            jax.ShapeDtypeStruct(w_dec.shape, F32),
+        ),
+        in_specs=[anywhere] * 3,
+        out_specs=[anywhere] + [vmem] * 3,
+        scratch_shapes=[
+            pltpu.VMEM(features.shape, BF),
+            pltpu.VMEM((n1, 80, 128), BF),
+            pltpu.VMEM((n2, 48, 128), BF),
+            dma((4,)),
+        ],
+        compiler_params=pltpu.CompilerParams(vmem_limit_bytes=60 * 2**20),
+    )(moved, a_sum, b_sum)
     return decoded, genc, gmid.transpose(0, 2, 1), gdec
 
 

time: 60.7 us -> 58.8 us (0.969)
  local copies, waits for them, and re-layouts: 4.83 us -> 0 us
  Pallas kernels: 54.9 us -> 58 us
    unnamed x10 -> x0, local copies, waits for them, and re-layouts: 4.83 us -> none
    pallas_call x1 -> x2, Pallas kernels: 54.9 us -> 58 us  [the longest x1 55.1 us: local(): pl.pallas_call(functools.partial(kernel, nz, ny), out_shape=(jax.ShapeDty...]
where the time goes in v2:
time: 58.8 us; the launch traced here: 58.7 us
  Pallas kernels  58 us (99%)
  between operations  0.64 us (1%)
    pallas_call x1, Pallas kernels, local(): pl.pallas_call(functools.partial(kernel, nz, ny), out_shape=(jax.ShapeDty...  55.1 us
    pallas_call x1, Pallas kernels, local(): pl.pallas_call(functools.partial(results, scale), out_shape=(jax.ShapeDty...  2.89 us

profile of v2, /device:TPU:41, one launch (start us, length us, event | category | flops | bytes accessed | tf_op | source)
XLA Modules:
  0.0 58.7 jit_solution(5495548414649944247)
XLA Ops:
  0.6 55.1 %shard_map.84 = (bf16[32,2,8,256]{3,2,1,0:T(8,128)(2,1)}, bf16[16,80,128]{2,1,0:T(8,128)(2,1)}, bf16[8,48,128]{2,1,0:T(8,128)(2,1)}) custom-call(bf16[32,2,8,256]{3,2,1,0:T(8,128)(2,1)} %feat_ref.1, bf16[32,2,8,256]{3,2,1,0:T(8,128)(2,1)} %cot_ref.1, bf16[27,32,32]{2,1,0:T(8,128)(2,1)} %wenc_hbm.1, bf16[27,32,64]{2,1,0:T(8,128)(2,1)} %bitcast.2, ...), custom_call_target="tpu_custom_call" | custom-call | tf_op jit(solution)/shard_map/pallas_call | solution.py:683
  55.8 2.9 %shard_map.85 = (bf16[32,2,8,256]{3,2,1,0:T(8,128)(2,1)}, f32[27,32,32]{2,1,0:T(8,128)}, f32[27,32,64]{2,1,0:T(8,128)}, f32[27,32,96]{2,1,0:T(8,128)}) custom-call(bf16[32,2,8,256]{3,2,1,0:T(8,128)(2,1)} %get-tuple-element.11.moved_hbm, bf16[16,80,128]{2,1,0:T(8,128)(2,1)} %get-tuple-element.12.a_hbm, bf16[8,48,128]{2,1,0:T(8,128)(2,1)} %get-tuple-element.13.b_hbm), custom_call_target="tpu_custom_call" | custom-call | tf_op jit(solution)/shard_map/pallas_call | solution.py:743

commit v3 on v2

--- a/solution.py
+++ b/solution.py
@@ -161,7 +161,8 @@
 
 
 class Total:
-    def __init__(self, first, second, mine, one, two, whole, sems):
+    def __init__(self, first, second, mine, one, two, whole, sems, final, fsem):
+        self.final, self.fsem = final, fsem
         self.first, self.second = first, second
         self.mine, self.one, self.two, self.whole = mine, one, two, whole
         self.send1, self.recv1, self.send2, self.recv2, self.send3, self.recv3 = sems
@@ -185,7 +186,7 @@
     def step3(self, t, incoming):
         g = self.first
         slot = t if incoming else g.me
-        return self.copy(self.whole.at[g.me], self.whole.at[slot], self.send3.at[t], self.recv3.at[slot], slot, g.peer(t))
+        return self.copy(self.final, self.whole.at[slot], self.send3.at[t], self.recv3.at[slot], slot, g.peer(t))
 
     def start1(self):
         for t in self.first.others():
@@ -206,11 +207,16 @@
         total = self.two[0].astype(F32)
         for t in range(1, self.second.size):
             total = total + self.two[t].astype(F32)
-        self.whole[self.first.me] = total.astype(BF)
+        self.final[...] = total.astype(BF)
+        self.keep().start()
         for t in self.first.others():
             self.step3(t, False).start()
 
+    def keep(self):
+        return pltpu.make_async_copy(self.final, self.whole.at[self.first.me], self.fsem)
+
     def finish(self):
+        self.keep().wait()
         for t in self.first.others():
             self.step3(t, True).wait_recv()
 
@@ -246,7 +252,7 @@
     fx, cx, sx, px, ox, bx,
     wenc_ref, wmid_ref, wdec_ref, wsem, we_ref, wm_ref, ws_ref, wc_ref, wb_ref, wp_ref, turned,
     slope, bskip, bsum, boxed, skips, benc, dec_acc, enc_acc, mid_acc, dplane,
-    a_mine, a_one, a_two, b_mine, b_one, b_two,
+    a_mine, a_one, a_two, b_mine, b_one, b_two, a_final, b_final, fsem,
     fin, cin, dout, msend, mrecv, hsend, hrecv, as1, ar1, as2, ar2, as3, ar3, bs1, br1, bs2, br2, bs3, br3,
 ):
     gz, gy = lax.axis_index("gz"), lax.axis_index("gy")
@@ -379,7 +385,6 @@
 
     lax.fori_loop(0, chigh, encode, 0)
     phalo.start()
-    shalo.start()
 
     chalo.arrived()
     four(ch, cx)
@@ -453,6 +458,7 @@
             bh[1, 1 + yc + p] = (silu_slope(cell) * bsum[yc + p]).astype(BF)
     bhalo.start()
     ohalo.start()
+    shalo.start()
 
     own = jnp.concatenate([oh[1, 1 + yc] for yc in range(chigh)], axis=1)
     none = jnp.zeros_like(own)
@@ -477,7 +483,7 @@
         piece = piece.astype(BF)
         for h in range(2):
             store(a_mine, 28 + 2 * d + h, piece[h * 16 : (h + 1) * 16])
-    a_total = Total(plane, column, a_mine, a_one, a_two, a_whole, (as1, ar1, as2, ar2, as3, ar3))
+    a_total = Total(plane, column, a_mine, a_one, a_two, a_whole, (as1, ar1, as2, ar2, as3, ar3), a_final, fsem.at[0])
     a_total.start1()
 
     bhalo.arrived()
@@ -500,7 +506,7 @@
 
     lax.fori_loop(0, chigh, encoder_grad, 0)
     pack(enc_acc, b_mine, 0)
-    b_total = Total(column, plane, b_mine, b_one, b_two, b_whole, (bs1, br1, bs2, br2, bs3, br3))
+    b_total = Total(column, plane, b_mine, b_one, b_two, b_whole, (bs1, br1, bs2, br2, bs3, br3), b_final, fsem.at[1])
     b_total.start1()
     a_total.start2()
 
@@ -688,7 +694,7 @@
             jax.ShapeDtypeStruct((n2, 48, 128), BF),
         ),
         in_specs=[anywhere] * 5,
-        out_specs=[anywhere] + [vmem] * 2,
+        out_specs=[anywhere] * 3,
         scratch_shapes=[
             pltpu.VMEM(fine + (c1, width), BF),
             pltpu.VMEM(fine + (c1, width), BF),
@@ -729,6 +735,9 @@
             pltpu.VMEM((n2, 48, 128), BF),
             pltpu.VMEM((n2, 48, 128), BF),
             pltpu.VMEM((n1, 48, 128), BF),
+            pltpu.VMEM((80, 128), BF),
+            pltpu.VMEM((48, 128), BF),
+            dma((2,)),
             pltpu.VMEM(features.shape, BF),
             pltpu.VMEM(features.shape, BF),
             pltpu.VMEM(features.shape, BF),

time: 58.8 us -> 57.8 us (0.983); the launches traced: 58.7 us -> 57 us
  Pallas kernels: 58 us -> 56.3 us
    pallas_call x1, Pallas kernels: 55.1 us -> 53.4 us  [local(): pl.pallas_call(functools.partial(kernel, nz, ny), out_shape=(jax.ShapeDty...]
where the time goes in v3:
time: 57.8 us; the launch traced here: 57 us
  Pallas kernels  56.3 us (97%)
  between operations  0.64 us (1%)
    pallas_call x1, Pallas kernels, local(): pl.pallas_call(functools.partial(kernel, nz, ny), out_shape=(jax.ShapeDty...  53.4 us
    pallas_call x1, Pallas kernels, local(): pl.pallas_call(functools.partial(results, scale), out_shape=(jax.ShapeDty...  2.89 us

profile of v3, /device:TPU:41, one launch (start us, length us, event | category | flops | bytes accessed | tf_op | source)
XLA Modules:
  0.0 57.0 jit_solution(10838108121528875164)
XLA Ops:
  0.6 53.4 %shard_map.84 = (bf16[32,2,8,256]{3,2,1,0:T(8,128)(2,1)}, bf16[16,80,128]{2,1,0:T(8,128)(2,1)}, bf16[8,48,128]{2,1,0:T(8,128)(2,1)}) custom-call(bf16[32,2,8,256]{3,2,1,0:T(8,128)(2,1)} %feat_ref.1, bf16[32,2,8,256]{3,2,1,0:T(8,128)(2,1)} %cot_ref.1, bf16[27,32,32]{2,1,0:T(8,128)(2,1)} %wenc_hbm.1, bf16[27,32,64]{2,1,0:T(8,128)(2,1)} %bitcast.2, ...), custom_call_target="tpu_custom_call" | custom-call | tf_op jit(solution)/shard_map/pallas_call | solution.py:689
  54.1 2.9 %shard_map.85 = (bf16[32,2,8,256]{3,2,1,0:T(8,128)(2,1)}, f32[27,32,32]{2,1,0:T(8,128)}, f32[27,32,64]{2,1,0:T(8,128)}, f32[27,32,96]{2,1,0:T(8,128)}) custom-call(bf16[32,2,8,256]{3,2,1,0:T(8,128)(2,1)} %get-tuple-element.11.moved_hbm, bf16[16,80,128]{2,1,0:T(8,128)(2,1)} %get-tuple-element.12.a_hbm, bf16[8,48,128]{2,1,0:T(8,128)(2,1)} %get-tuple-element.13.b_hbm), custom_call_target="tpu_custom_call" | custom-call | tf_op jit(solution)/shard_map/pallas_call | solution.py:752
